TPU v7x, 32 devices: a whole 2x2x4 slice. The times are simulated.
32 devices in a mesh: grp: 2 (over y), tm: 4 (over z), feat: 2 (over x), rep: 2 (over core).
Axes of the slice: x: 2, y: 2, z: 4, core: 2. Of those that a mesh axis runs over, the one named last changes fastest.
Arguments:
- archive: float32 [128, 4, 3, 4096], P(('grp', 'tm'), ('feat', 'rep')), parts along dimension 0
- swap_history: int32 [128, 4], P(('grp', 'tm')), parts along dimension 0, may hold values from 0 to 3, as said below
- pair_index: int32 [2, 4096], replicated, may hold values from 0 to 4095
Outputs:
- inst_cov: float32 [8192, 4096], P(('grp', 'tm'), ('feat', 'rep')), parts along dimension 0
- lag_cov: float32 [8192, 4096], P(('grp', 'tm'), ('feat', 'rep')), parts along dimension 0
There are 2 independent parts, one for each index of `grp`. A program takes and returns all parts, laid end to end along the dimension named above; an argument that names none is the same for every part. Nothing has to cross between parts.
Inputs may be any that keep to these rules, and one draw needn't show every extreme that they name: Each row swap_history[t, :] is a permutation of 0 to 3.
All inputs are finite; a program needn't handle non-finite values.
Results may differ from a plain program's by a relative error of at most 0.0027.
Values may be sent and summed in bfloat16 or wider, within the bound.
A program may use at most 128 MiB of HBM per device.

v0:
```python
import jax
import jax.numpy as jnp
from jax import lax
from jax.sharding import PartitionSpec as P

LAG = 16


DIST_FLOOR = 0.3


def shifted(block, axis, distance):
    devices = range(lax.axis_size(axis))
    route = [(i - distance, i) for i in devices if i - distance in devices]
    return lax.ppermute(block, axis, route)


def featurize(coords, pair_index):
    coords_one = jnp.take(coords, pair_index[0], axis=-1)
    coords_two = jnp.take(coords, pair_index[1], axis=-1)
    displace = coords_one - coords_two
    distance = jnp.sqrt(jnp.sum(displace * displace, axis=-2))
    return (1.0 / jnp.maximum(distance, DIST_FLOOR)).astype(jnp.bfloat16)


def holder_states(swap_rows, replicas):
    wanted = jnp.arange(replicas, dtype=jnp.int32)
    matches = swap_rows[:, :, None] == wanted[None, None, :]
    states = jnp.arange(replicas, dtype=jnp.int32)[None, :, None]
    return jnp.sum(jnp.where(matches, states, 0), axis=1)


def to_replicas(frames, inverse):
    expanded = inverse.reshape(inverse.shape + (1,) * (frames.ndim - 2))
    expanded = jnp.broadcast_to(expanded, frames.shape)
    return jnp.take_along_axis(frames, expanded, axis=1)


def local(archive, swap_history, pair_index):
    steps_tm = archive.shape[0]
    groups = lax.axis_size(("feat", "rep"))
    tm_count = lax.axis_size("tm")
    replicas = archive.shape[1] * groups
    sub_steps = steps_tm // groups
    group_idx = lax.axis_index(("feat", "rep"))
    time_idx = lax.axis_index("tm")
    own_swaps = lax.dynamic_slice_in_dim(swap_history, group_idx * sub_steps, sub_steps, 0)
    inverse = holder_states(own_swaps, replicas)
    state_feats = featurize(archive, pair_index)
    features = lax.all_to_all(
        to_replicas(
            lax.all_to_all(state_feats, ("feat", "rep"), split_axis=0, concat_axis=1, tiled=True),
            inverse,
        ),
        ("feat", "rep"),
        split_axis=1,
        concat_axis=0,
        tiled=True,
    )
    by_replica = jnp.swapaxes(features, 0, 1)
    kept_steps = steps_tm * tm_count - LAG
    frame_count = kept_steps * replicas
    step_ids = time_idx * steps_tm + jnp.arange(steps_tm, dtype=jnp.int32)
    lead_rows = jnp.where(
        (step_ids < kept_steps)[None, :, None], by_replica, jnp.zeros_like(by_replica)
    )
    row_mid = lax.all_to_all(lead_rows, "tm", split_axis=2, concat_axis=1, tiled=True)
    next_lead = shifted(by_replica, "tm", -1)
    lagged = jnp.concatenate([by_replica[:, LAG:], next_lead], axis=1)
    col_lead, col_lag = (
        lax.all_to_all(by_replica, ("feat", "rep"), split_axis=2, concat_axis=0, tiled=True),
        lax.all_to_all(lagged, ("feat", "rep"), split_axis=2, concat_axis=0, tiled=True),
    )
    lead_cols, lag_cols = (
        lax.all_gather(col_lead, "tm", axis=1, tiled=True),
        lax.all_gather(col_lag, "tm", axis=1, tiled=True),
    )
    mean_lead_cols = (
        jnp.sum(lead_cols[:, :kept_steps], axis=(0, 1), dtype=jnp.float32) / frame_count
    )
    mean_lag_cols = jnp.sum(lag_cols[:, :kept_steps], axis=(0, 1), dtype=jnp.float32) / frame_count
    portion = lax.all_gather(row_mid, ("feat", "rep"), axis=0, tiled=True)
    inst_sum = jnp.einsum("rta,rtb->ab", portion, lead_cols, preferred_element_type=jnp.float32)
    lag_sum = jnp.einsum("rta,rtb->ab", portion, lag_cols, preferred_element_type=jnp.float32)
    row_sum = jnp.sum(portion, axis=(0, 1), dtype=jnp.float32)
    inst_sum, lag_sum, row_sum = (inst_sum, lag_sum, row_sum)
    mean_lead_rows = row_sum / frame_count
    inst_cov = inst_sum / frame_count - mean_lead_rows[:, None] * mean_lead_cols[None, :]
    lag_cov = lag_sum / frame_count - mean_lead_rows[:, None] * mean_lag_cols[None, :]
    return (inst_cov, lag_cov)


def solution(mesh):
    placed = (P(("grp", "tm"), ("feat", "rep"), None, None), P(("grp", "tm"), None), P())
    return jax.shard_map(
        local,
        mesh=mesh,
        in_specs=placed,
        out_specs=(P(("grp", "tm"), ("feat", "rep")), P(("grp", "tm"), ("feat", "rep"))),
        check_vma=False,
    )
```

profile of v0, /device:TPU:0, one launch (start us, length us, event | category | flops | bytes accessed | tf_op | source)
XLA Modules:
  0.0 914.5 jit_solution(12617092971072731062)
XLA Ops:
  1.6 1.6 copy.97
  3.2 5.9 copy.75
  9.0 33.5 %gather_fusion.2 = f32[4096,16,3]{1,2,0:T(4,128)} fusion(f32[16,3,4096]{0,1,2:T(4,128)} %copy.75, s32[4096]{0:T(1024)S(1)} %fusion.9), kind=kCustom, calls=%fused_computation.1.clone | custom fusion | bytes 1589248 | tf_op jit(solution)/shard_map/jit(_take)/gather | solution.py:20
  42.6 33.5 %gather_fusion.1 = f32[4096,16,3]{1,2,0:T(4,128)} fusion(f32[16,3,4096]{0,1,2:T(4,128)} %copy.75, s32[4096]{0:T(1024)S(1)} %fusion.8), kind=kCustom, calls=%fused_computation.clone | custom fusion | bytes 1589248 | tf_op jit(solution)/shard_map/jit(_take)/gather | solution.py:19
  76.1 25.7 %fusion.2 = f32[16,4096]{0,1:T(8,128)S(1)} fusion(f32[4096,16,3]{1,2,0:T(4,128)} %gather_fusion.2, f32[4096,16,3]{1,2,0:T(4,128)} %gather_fusion.1, pred[4096]{0:T(1024)(128)(4,1)S(1)} %get-tuple-element.5, pred[4096]{0:T(1024)(128)(4,1)S(1)} %get-tuple-element.6), kind=kLoop, calls=%fused_computation.6 | loop fusion | flops 917504 | bytes 1843200 | tf_op jit(solution)/shard_map/reduce_sum | solution.py:22
  104.4 4.2 all-to-all-start
  109.0 4.2 all-to-all-done
  114.2 634.9 %gather_fusion = bf16[65536]{0:T(1024)(128)(2,1)S(1)} fusion(bf16[4,4,4096]{2,0,1:T(4,128)(2,1)S(1)} %bitcast.74, s32[65536]{0:T(1024)S(1)} %bitcast.75), kind=kCustom, calls=%fused_computation.2 | custom fusion | bytes 1048576 | tf_op jit(solution)/shard_map/jit(take_along_axis)/gather | solution.py:36
  750.0 3.3 all-to-all-start.1
  753.4 4.6 all-to-all-done.1
  758.0 2.7 copy.84
  762.2 22.3 %reduce.4 = bf16[4096,16]{1,0:T(8,128)(2,1)S(1)} reduce(bf16[4096,1,16]{2,1,0:T(2,128)(2,1)S(1)} %bitcast.76, bf16[]{:T(256)} %broadcast.178), dimensions={1}, to_apply=%bitcast.63.reduce_sub_computation | reduce | bytes 262146
  784.6 1.7 reshape.149
  786.3 3.5 all-to-all-start.3
  789.9 2.7 copy.81
  792.7 22.3 %reduce.3 = bf16[4096,16]{1,0:T(8,128)(2,1)S(1)} reduce(bf16[4096,1,16]{2,1,0:T(2,128)(2,1)S(1)} %bitcast.78, bf16[]{:T(256)} %broadcast.178), dimensions={1}, to_apply=%bitcast.61.reduce_sub_computation | reduce | bytes 262146
  815.0 1.7 reshape.147
  816.8 6.9 all-to-all-start.2
  825.2 2.0 copy.85
  827.2 16.3 %all-gather = bf16[4,1,64,1024]{3,2,0,1:T(8,128)(2,1)S(1)} all-gather(bf16[4,1,16,1024]{3,2,0,1:T(8,128)(2,1)S(1)} %bitcast.86), channel_id=2, replica_groups=mesh['grp'=2,'tm'=4,'feat'=2,'rep'=2] {'tm'}, dimensions={2}, use_global_device_ids=true | all-gather | bytes 655360 | tf_op jit(solution)/shard_map/all_gather | solution.py:75
  844.3 4.3 copy.87
  848.6 22.3 %reduce.5 = bf16[4096,16]{1,0:T(8,128)(2,1)S(1)} reduce(bf16[4096,1,16]{2,1,0:T(2,128)(2,1)S(1)} %bitcast.77, bf16[]{:T(256)} %broadcast.178), dimensions={1}, to_apply=%bitcast.65.reduce_sub_computation | reduce | bytes 262146
  870.9 1.7 reshape.151
  872.7 3.3 all-to-all-start.4
  876.0 1.5 reshape.148
  877.5 2.0 copy.82
  879.6 7.7 all_gather.9
  887.4 3.8 fusion.4
  891.3 1.5 reshape.152
  892.8 2.0 copy.88
  894.8 16.9 %all-gather.1 = bf16[4,1,64,1024]{3,2,0,1:T(8,128)(2,1)S(1)} all-gather(bf16[4,1,16,1024]{3,2,0,1:T(8,128)(2,1)S(1)} %bitcast.89), channel_id=3, replica_groups=mesh['grp'=2,'tm'=4,'feat'=2,'rep'=2] {'tm'}, dimensions={2}, use_global_device_ids=true | all-gather | bytes 655360 | tf_op jit(solution)/shard_map/all_gather | solution.py:76
  911.7 2.8 fusion.3
  (45 shorter events, 10.0 us)
Async XLA Ops:
  0.6 108.0 %copy-start = (s32[16,4]{0,1:T(4,128)S(1)}, s32[16,4]{0,1:T(4,128)}, u32[]{:S(2)}) copy-start(s32[16,4]{0,1:T(4,128)} %param.6) | copy-start | bytes 772
  104.4 8.8 all-to-all-start
  750.0 7.9 all-to-all-start.1
  760.7 83.5 %collective-permute-start = (bf16[1,16,4096]{2,1,0:T(8,128)(2,1)S(1)}, bf16[1,16,4096]{2,1,0:T(8,128)(2,1)}, u32[]{:S(2)}, u32[]{:S(2)}) collective-permute-start(bf16[1,16,4096]{2,1,0:T(8,128)(2,1)S(1)} %transpose.11), channel_id=1, source_target_pairs={{4,0},{8,4},{12,8},{5,1},{9,5},{13,9},{6,2},{10,6},{14,10},{7,3},{... | collective-permute-start | bytes 393224 | tf_op jit(solution)/shard_map/ppermute | solution.py:15
  786.3 30.5 %all-to-all-start.3 = ((bf16[4,2,8192]{2,1,0:T(2,128)(2,1)}), bf16[4,2,8192]{2,1,0:T(2,128)(2,1)S(1)}, u32[]{:S(2)}, u32[]{:S(2)}) async-start(bf16[4,2,8192]{2,1,0:T(2,128)(2,1)} %reshape.149), calls=%async_computation.3 | async-start | bytes 262144 | tf_op jit(solution)/shard_map/all_to_all | solution.py:71
  816.8 55.9 %all-to-all-start.2 = ((bf16[4,2,8192]{2,1,0:T(2,128)(2,1)}), bf16[4,2,8192]{2,1,0:T(2,128)(2,1)S(1)}, u32[]{:S(2)}, u32[]{:S(2)}) async-start(bf16[4,2,8192]{2,1,0:T(2,128)(2,1)} %reshape.147), calls=%async_computation.2 | async-start | bytes 262144 | tf_op jit(solution)/shard_map/all_to_all | solution.py:67
  843.5 0.8 copy-start.1
  872.7 18.6 %all-to-all-start.4 = ((bf16[4,2,8192]{2,1,0:T(2,128)(2,1)}), bf16[4,2,8192]{2,1,0:T(2,128)(2,1)S(1)}, u32[]{:S(2)}, u32[]{:S(2)}) async-start(bf16[4,2,8192]{2,1,0:T(2,128)(2,1)} %reshape.151), calls=%async_computation.4 | async-start | bytes 262144 | tf_op jit(solution)/shard_map/all_to_all | solution.py:72
where the time goes:
time: 916 us; the launch traced here: 915 us
  local copies, waits for them, and re-layouts  740 us (81%)
  other arithmetic  94.9 us (10%)
  blocking collectives  40.8 us (4%)
  starting transfers between devices  22.8 us (2%)
    gather x2, local copies, waits for them, and re-layouts, to_replicas(): return jnp.take_along_axis(frames, expanded, axis=1)  635 us
    unnamed x4, other arithmetic  67.1 us
    gather x1, local copies, waits for them, and re-layouts, featurize(): coords_one = jnp.take(coords, pair_index[0], axis=-1)  33.5 us
    gather x1, local copies, waits for them, and re-layouts, featurize(): coords_two = jnp.take(coords, pair_index[1], axis=-1)  33.5 us
    reduce_sum x1, other arithmetic, featurize(): distance = jnp.sqrt(jnp.sum(displace * displace, axis=-2))  25.7 us
  transfers between devices with their start and end apart: 6, of which 2 were waited for; matrix products, arithmetic and copies ran while one was open for 10% of the time, Pallas kernels for 0%

commit v1 on v0

v1 whole, which is shorter than its diff:
```python
import functools

import jax
import jax.numpy as jnp
from jax import lax
from jax.experimental import pallas as pl
from jax.experimental.pallas import tpu as pltpu
from jax.sharding import PartitionSpec as P

LAG = 16
DIST_FLOOR = 0.3
LANES = 128
SUBLANES = 8
MESH = pl.DeviceIdType.MESH
BF16, F32, I32 = jnp.bfloat16, jnp.float32, jnp.int32


def lane_pick(table, lanes):
    return jnp.take_along_axis(table, lanes, axis=1, mode="promise_in_bounds")


def feature_tile(x_ref, idx_ref, start):
    steps, residues = x_ref.shape[1:]
    groups = [(c, t) for c in range(3) for t in range(0, steps, SUBLANES)]
    lanes, chunks = [], []
    for side in range(2):
        index = jnp.broadcast_to(idx_ref[side : side + 1, pl.ds(start, LANES)], (SUBLANES, LANES))
        lanes.append(lax.bitwise_and(index, LANES - 1))
        chunks.append(lax.shift_right_logical(index, 7))
    picked = [[None] * len(groups) for _ in range(2)]
    for chunk in range(residues // LANES):
        masks = [chunks[side] == chunk for side in range(2)]
        for g, (c, t) in enumerate(groups):
            table = x_ref[c, t : t + SUBLANES, chunk * LANES : (chunk + 1) * LANES]
            for side in range(2):
                found = lane_pick(table, lanes[side])
                old = picked[side][g]
                picked[side][g] = found if old is None else jnp.where(masks[side], found, old)
    halves = steps // SUBLANES
    out = []
    for h in range(halves):
        total = None
        for c in range(3):
            g = c * halves + h
            diff = picked[0][g] - picked[1][g]
            total = diff * diff if total is None else total + diff * diff
        out.append(1.0 / jnp.maximum(jnp.sqrt(total), DIST_FLOOR))
    return jnp.concatenate(out, axis=0).astype(BF16)


def feature_kernel(x_ref, idx_ref, out_ref):
    blocks, _, width = out_ref.shape
    tiles = width // LANES

    def tile(q, carry):
        b, within = q // tiles, (q % tiles) * LANES
        start = pl.multiple_of(q * LANES, LANES)
        out_ref[b, :, pl.ds(pl.multiple_of(within, LANES), LANES)] = feature_tile(x_ref, idx_ref, start)
        return carry

    lax.fori_loop(0, blocks * tiles, tile, 0)


def exchange_kernel(n, n_rep, feat_ref, swap_ref, rows_ref, cols_ref, swaps_ref,
                    s_row1, r_row1, s_col1, r_col1, s_row2, r_row2, s_col2, r_col2, s_sw, r_sw, own_sem):
    i0 = lax.axis_index("tm")
    g0 = lax.axis_index("feat") * n_rep + lax.axis_index("rep")
    is_lead = i0 < n - 1

    def time_id(i):
        return {"tm": i}

    def group_id(j):
        return {"feat": j // n_rep, "rep": j % n_rep}

    def others(me, body):
        def step(d, carry):
            body((me + d) % n)
            return carry
        lax.fori_loop(1, n, step, 0)

    def remote(src, dst, send, recv, device):
        return pltpu.make_async_remote_copy(
            src_ref=src, dst_ref=dst, send_sem=send, recv_sem=recv, device_id=device, device_id_type=MESH)

    def row1(i):
        return remote(feat_ref.at[i], rows_ref.at[i0, g0], s_row1.at[i], r_row1.at[i0], time_id(i))

    def row1_in(i):
        return remote(feat_ref.at[i0], rows_ref.at[i, g0], s_row1.at[i], r_row1.at[i], time_id(i))

    def col1(j):
        return remote(feat_ref.at[j], cols_ref.at[i0, g0], s_col1.at[j], r_col1.at[g0], group_id(j))

    def col1_in(j):
        return remote(feat_ref.at[g0], cols_ref.at[i0, j], s_col1.at[j], r_col1.at[j], group_id(j))

    def row2(i, j):
        return remote(rows_ref.at[i, g0], rows_ref.at[i, g0], s_row2.at[i, j], r_row2.at[i, g0], group_id(j))

    def row2_in(i, j):
        return remote(rows_ref.at[i, j], rows_ref.at[i, j], s_row2.at[i, j], r_row2.at[i, j], group_id(j))

    def col2(i, j):
        return remote(cols_ref.at[i0, j], cols_ref.at[i0, j], s_col2.at[i, j], r_col2.at[i0, j], time_id(i))

    def col2_in(i, j):
        return remote(cols_ref.at[i, j], cols_ref.at[i, j], s_col2.at[i, j], r_col2.at[i, j], time_id(i))

    def swap(i):
        return remote(swap_ref, swaps_ref.at[i0], s_sw.at[i], r_sw.at[i0], time_id(i))

    def swap_in(i):
        return remote(swap_ref, swaps_ref.at[i], s_sw.at[i], r_sw.at[i], time_id(i))

    barrier = pltpu.get_barrier_semaphore()
    others(i0, lambda i: pl.semaphore_signal(barrier, inc=1, device_id=time_id(i), device_id_type=MESH))
    others(g0, lambda j: pl.semaphore_signal(barrier, inc=1, device_id=group_id(j), device_id_type=MESH))
    pl.semaphore_wait(barrier, 2 * (n - 1))

    others(g0, lambda j: col1(j).start())

    @pl.when(is_lead)
    def _():
        others(i0, lambda i: row1(i).start())

    own_col = pltpu.make_async_copy(feat_ref.at[g0], cols_ref.at[i0, g0], own_sem.at[0])
    own_sw = pltpu.make_async_copy(swap_ref, swaps_ref.at[i0], own_sem.at[2])
    own_col.start()
    own_sw.start()
    others(i0, lambda i: swap(i).start())

    @pl.when(is_lead)
    def _():
        own_row = pltpu.make_async_copy(feat_ref.at[i0], rows_ref.at[i0, g0], own_sem.at[1])
        own_row.start()
        own_row.wait()
        others(g0, lambda j: row2(i0, j).start())

    own_col.wait()
    others(i0, lambda i: col2(i, g0).start())

    def forward_col(j):
        col1_in(j).wait_recv()
        others(i0, lambda i: col2(i, j).start())

    others(g0, forward_col)

    def forward_row(i):
        @pl.when(i < n - 1)
        def _():
            row1_in(i).wait_recv()
            others(g0, lambda j: row2(i, j).start())

    others(i0, forward_row)

    own_sw.wait()

    def finish_swap(i):
        swap_in(i).wait_recv()
        swap(i).wait_send()

    others(i0, finish_swap)
    others(g0, lambda j: col1(j).wait_send())

    @pl.when(is_lead)
    def _():
        others(i0, lambda i: row1(i).wait_send())

    def end_rows(i, carry):
        def one(j):
            row2(i, j).wait_send()
            row2_in(i, j).wait_recv()
        others(g0, one)
        return carry

    lax.fori_loop(0, n - 1, end_rows, 0)

    def end_cols(j, carry):
        def one(i):
            col2(i, j).wait_send()
            col2_in(i, j).wait_recv()
        others(i0, one)
        return carry

    lax.fori_loop(0, n, end_cols, 0)


def covariance_kernel(frames, rows_ref, cols_ref, swaps_ref, inst_ref, lag_ref, lagged_ref, means_ref):
    blocks, per, _ = cols_ref.shape
    lead_rows = (blocks - 1) * per
    kept = lead_rows
    scale = 1.0 / frames

    @pl.when(pl.program_id(0) == 0)
    def _():
        here = lax.broadcasted_iota(I32, (per, per), 0) % LAG
        there = lax.broadcasted_iota(I32, (per, per), 1) % LAG
        same_step = here == there
        for i in range(blocks - 1):
            now = jnp.broadcast_to(swaps_ref[i, 0:1, :], (per, per)).T
            later = jnp.broadcast_to(swaps_ref[i + 1, 0:1, :], (per, per))
            pairs = jnp.where(same_step & (now == later), 1.0, 0.0).astype(BF16)
            lagged_ref[i * per : (i + 1) * per, :] = jnp.dot(
                pairs, cols_ref[i + 1], preferred_element_type=F32).astype(BF16)
        ones = jnp.ones((SUBLANES, kept), BF16)
        lead = cols_ref[: blocks - 1].reshape(kept, cols_ref.shape[2])
        means_ref[0] = jnp.dot(ones, lead, preferred_element_type=F32) * scale
        means_ref[1] = jnp.dot(ones, lagged_ref[...], preferred_element_type=F32) * scale

    rows = rows_ref[...].reshape(kept, rows_ref.shape[2])
    lead = cols_ref[: blocks - 1].reshape(kept, cols_ref.shape[2])
    contract = (((0,), (0,)), ((), ()))
    row_mean = lax.dot_general(rows, jnp.ones((kept, LANES), BF16), contract, preferred_element_type=F32)
    row_mean = row_mean[:, :1] * scale
    inst = lax.dot_general(rows, lead, contract, preferred_element_type=F32)
    inst_ref[...] = inst * scale - row_mean * means_ref[0, 0:1, :]
    lag = lax.dot_general(rows, lagged_ref[...], contract, preferred_element_type=F32)
    lag_ref[...] = lag * scale - row_mean * means_ref[1, 0:1, :]


def vmem(count):
    return [pl.BlockSpec(memory_space=pltpu.VMEM)] * count


def solution(mesh):
    n = mesh.shape["tm"]
    n_rep = mesh.shape["rep"]

    def local(archive, swap_history, pair_index):
        steps, _, _, residues = archive.shape
        feats = pair_index.shape[1]
        width = feats // n
        per = n * steps
        x = jnp.swapaxes(archive[:, 0], 0, 1)
        swap = jnp.broadcast_to(swap_history.T.reshape(1, per).astype(F32), (SUBLANES, per))
        features = pl.pallas_call(
            feature_kernel,
            out_shape=jax.ShapeDtypeStruct((n, steps, width), BF16),
            in_specs=vmem(2),
            out_specs=vmem(1)[0],
            compiler_params=pltpu.CompilerParams(vmem_limit_bytes=32 << 20),
        )(x, pair_index)
        dma = pltpu.SemaphoreType.DMA
        rows, cols, swaps = pl.pallas_call(
            functools.partial(exchange_kernel, n, n_rep),
            out_shape=[
                jax.ShapeDtypeStruct((n - 1, n, steps, width), BF16),
                jax.ShapeDtypeStruct((n, n, steps, width), BF16),
                jax.ShapeDtypeStruct((n, SUBLANES, per), F32),
            ],
            in_specs=vmem(2),
            out_specs=vmem(3),
            scratch_shapes=[dma((n,)), dma((n,)), dma((n,)), dma((n,)),
                            dma((n, n)), dma((n, n)), dma((n, n)), dma((n, n)),
                            dma((n,)), dma((n,)), dma((3,))],
            compiler_params=pltpu.CompilerParams(
                collective_id=0, has_side_effects=True, vmem_limit_bytes=32 << 20),
        )(features, swap)
        tile = min(256, width)
        shape = jax.ShapeDtypeStruct((width, width), F32)
        return pl.pallas_call(
            functools.partial(covariance_kernel, (n - 1) * per),
            grid=(width // tile,),
            out_shape=[shape, shape],
            in_specs=[
                pl.BlockSpec((n - 1, per, tile), lambda r: (0, 0, r)),
                pl.BlockSpec((n, per, width), lambda r: (0, 0, 0)),
                pl.BlockSpec((n, SUBLANES, per), lambda r: (0, 0, 0)),
            ],
            out_specs=[pl.BlockSpec((tile, width), lambda r: (r, 0))] * 2,
            scratch_shapes=[pltpu.VMEM(((n - 1) * per, width), BF16), pltpu.VMEM((2, SUBLANES, width), F32)],
            compiler_params=pltpu.CompilerParams(vmem_limit_bytes=48 << 20),
        )(rows.reshape(n - 1, per, width), cols.reshape(n, per, width), swaps)

    return jax.shard_map(
        local,
        mesh=mesh,
        in_specs=(P(("grp", "tm"), ("feat", "rep"), None, None), P(("grp", "tm"), None), P()),
        out_specs=(P(("grp", "tm"), ("feat", "rep")), P(("grp", "tm"), ("feat", "rep"))),
        check_vma=False,
    )
```

time: 916 us -> 44.8 us (0.05)
  local copies, waits for them, and re-layouts: 740 us -> 2.43 us
  other arithmetic: 94.9 us -> 0.68 us
  blocking collectives: 40.8 us -> 0 us
  Pallas kernels: 0 us -> 40.7 us
  starting transfers between devices: 22.8 us -> 0 us
    gather x4 -> x0, local copies, waits for them, and re-layouts: 702 us -> none  [the longest x2 635 us: to_replicas(): return jnp.take_along_axis(frames, expanded, axis=1)]
    unnamed x4 -> x0, other arithmetic: 67.1 us -> none
    all_gather x3 -> x0, blocking collectives: 40.8 us -> none  [the longest x1 16.9 us: local(): lax.all_gather(col_lag, 'tm', axis=1, tiled=True)]
    pallas_call x0 -> x3, Pallas kernels: none -> 40.7 us  [the longest x1 20.1 us: local(): pl.pallas_call(functools.partial(exchange_kernel, n, n_rep), out_shape=[j...]
    reduce_sum x5 -> x0, other arithmetic: 26 us -> none  [the longest x1 25.7 us: featurize(): distance = jnp.sqrt(jnp.sum(displace * displace, axis=-2))]
    all_to_all x5 -> x0, starting transfers between devices: 21.3 us -> none  [the longest x1 6.93 us: local(): lax.all_to_all(lead_rows, 'tm', split_axis=2, concat_axis=1, tiled=True)]
    unnamed x14 -> x3, local copies, waits for them, and re-layouts: 13 us -> 2.34 us
  transfers between devices with their start and end apart: 6 -> 0, of which waited for: 2 -> 0; matrix products, arithmetic and copies ran while one was open for 10% -> 0% of each run, Pallas kernels for 0% -> 0%
where the time goes in v1:
time: 44.8 us; the launch traced here: 44.5 us
  Pallas kernels  40.7 us (91%)
  local copies, waits for them, and re-layouts  2.43 us (5%)
  other arithmetic  0.68 us (2%)
  between operations  0.66 us (1%)
    pallas_call x1, Pallas kernels, local(): pl.pallas_call(functools.partial(exchange_kernel, n, n_rep), out_shape=[j...  20.1 us
    pallas_call x1, Pallas kernels, local(): pl.pallas_call(feature_kernel, out_shape=jax.ShapeDtypeStruct((n, steps,...  16 us
    pallas_call x1, Pallas kernels, local(): pl.pallas_call(functools.partial(covariance_kernel, (n - 1) * per), grid=...  4.57 us
    unnamed x3, local copies, waits for them, and re-layouts  2.34 us

profile of v1, /device:TPU:0, one launch (start us, length us, event | category | flops | bytes accessed | tf_op | source)
XLA Modules:
  0.0 44.5 jit_solution(17203930708453890689)
XLA Ops:
  0.6 0.7 %convert_bitcast_fusion = f32[4,16]{1,0:T(4,128)S(1)} fusion(s32[16,4]{0,1:T(4,128)} %param.4), kind=kLoop, calls=%fused_computation.1 | loop fusion | flops 64 | bytes 512 | tf_op jit(solution)/shard_map/convert_element_type | solution.py:236
  1.3 0.1 convert_element_type.16
  1.4 1.6 %copy.7 = f32[16,1,3,4096]{3,0,2,1:T(8,128)S(1)} copy(f32[16,1,3,4096]{3,1,2,0:T(1,128)} %param.3) | data formatting | bytes 1572864 | tf_op args[0]
  3.0 0.0 copy-start
  3.0 0.7 %copy-done = s32[2,4096]{1,0:T(2,128)S(1)} copy-done((s32[2,4096]{1,0:T(2,128)S(1)}, s32[2,4096]{1,0:T(2,128)}, u32[]{:S(2)}) %copy-start) | copy-done | bytes 32792
  3.8 16.0 %shard_map.50.feat_ref = bf16[4,16,1024]{2,1,0:T(8,128)(2,1)S(1)} custom-call(f32[3,16,4096]{2,1,0:T(8,128)S(1)} %bitcast.9, s32[2,4096]{1,0:T(2,128)S(1)} %copy-done), custom_call_target="tpu_custom_call" | custom-call | tf_op jit(solution)/shard_map/pallas_call | solution.py:237
  19.8 20.1 %shard_map.51 = (bf16[3,4,16,1024]{3,2,1,0:T(8,128)(2,1)S(1)}, bf16[4,4,16,1024]{3,2,1,0:T(8,128)(2,1)S(1)}, f32[4,8,64]{2,1,0:T(8,128)S(1)}) custom-call(bf16[4,16,1024]{2,1,0:T(8,128)(2,1)S(1)} %shard_map.50.feat_ref, f32[8,64]{1,0:T(8,128)S(1)} %broadcast_in_dim.2.swap_ref), custom_call_target="tpu_custom_call" | custom-call | tf_op jit(solution)/shard_map/pallas_call | solution.py:245
  39.9 4.6 %shard_map.52 = (f32[1024,1024]{1,0:T(8,128)}, f32[1024,1024]{1,0:T(8,128)}) custom-call(bf16[3,64,1024]{2,1,0:T(8,128)(2,1)S(1)} %bitcast.11, bf16[4,64,1024]{2,1,0:T(8,128)(2,1)S(1)} %bitcast.10, f32[4,8,64]{2,1,0:T(8,128)S(1)} %get-tuple-element.7.swaps_ref), custom_call_target="tpu_custom_call" | custom-call | tf_op jit(solution)/shard_map/pallas_call | solution.py:262
  (1 shorter events, 0.0 us)
Async XLA Ops:
  3.0 0.8 %copy-start = (s32[2,4096]{1,0:T(2,128)S(1)}, s32[2,4096]{1,0:T(2,128)}, u32[]{:S(2)}) copy-start(s32[2,4096]{1,0:T(2,128)} %idx_ref.1) | copy-start | bytes 98308

commit v2 on v1

--- a/solution.py
+++ b/solution.py
@@ -48,24 +48,28 @@
     return jnp.concatenate(out, axis=0).astype(BF16)
 
 
-def feature_kernel(x_ref, idx_ref, out_ref):
-    blocks, _, width = out_ref.shape
-    tiles = width // LANES
-
-    def tile(q, carry):
-        b, within = q // tiles, (q % tiles) * LANES
-        start = pl.multiple_of(q * LANES, LANES)
-        out_ref[b, :, pl.ds(pl.multiple_of(within, LANES), LANES)] = feature_tile(x_ref, idx_ref, start)
-        return carry
-
-    lax.fori_loop(0, blocks * tiles, tile, 0)
-
-
-def exchange_kernel(n, n_rep, feat_ref, swap_ref, rows_ref, cols_ref, swaps_ref,
+def flat_swaps(swap):
+    states, steps = swap.shape
+    per = steps * states
+    lane = lax.broadcasted_iota(I32, (steps, per), 1)
+    spread = jnp.where(lane % steps == lax.broadcasted_iota(I32, (steps, per), 0), 1.0, 0.0)
+    wide = jnp.dot(swap.astype(F32).astype(BF16), spread.astype(BF16), preferred_element_type=F32)
+    lane = lax.broadcasted_iota(I32, (states, per), 1)
+    mine = lane // steps == lax.broadcasted_iota(I32, (states, per), 0)
+    row = jnp.sum(jnp.where(mine, wide, 0.0), axis=0, keepdims=True)
+    return jnp.broadcast_to(row, (SUBLANES, per))
+
+
+def exchange_kernel(n, n_rep, raw_ref, idx_hbm, swap_in_ref, rows_ref, cols_ref, swaps_ref,
+                    raw, idx_ref, x_ref, feat_ref, swap_ref,
                     s_row1, r_row1, s_col1, r_col1, s_row2, r_row2, s_col2, r_col2, s_sw, r_sw, own_sem):
     i0 = lax.axis_index("tm")
     g0 = lax.axis_index("feat") * n_rep + lax.axis_index("rep")
     is_lead = i0 < n - 1
+    get_raw = pltpu.make_async_copy(raw_ref, raw, own_sem.at[0])
+    get_idx = pltpu.make_async_copy(idx_hbm, idx_ref, own_sem.at[1])
+    get_raw.start()
+    get_idx.start()
 
     def time_id(i):
         return {"tm": i}
@@ -116,45 +120,72 @@
     barrier = pltpu.get_barrier_semaphore()
     others(i0, lambda i: pl.semaphore_signal(barrier, inc=1, device_id=time_id(i), device_id_type=MESH))
     others(g0, lambda j: pl.semaphore_signal(barrier, inc=1, device_id=group_id(j), device_id_type=MESH))
+
+    swap_ref[...] = flat_swaps(swap_in_ref[...])
+    swaps_ref[i0] = swap_ref[...]
+    _, steps, residues = x_ref.shape
+    chunks = residues // LANES
+    width = feat_ref.shape[2]
+    get_raw.wait()
+    for c in range(3):
+        for t in range(0, steps, SUBLANES):
+            for h in range(chunks):
+                x_ref[c, t : t + SUBLANES, h * LANES : (h + 1) * LANES] = raw[
+                    pl.ds((t * 3 + c) * chunks + h, SUBLANES, stride=3 * chunks), :]
+    get_idx.wait()
     pl.semaphore_wait(barrier, 2 * (n - 1))
-
-    others(g0, lambda j: col1(j).start())
-
-    @pl.when(is_lead)
-    def _():
-        others(i0, lambda i: row1(i).start())
-
-    own_col = pltpu.make_async_copy(feat_ref.at[g0], cols_ref.at[i0, g0], own_sem.at[0])
-    own_sw = pltpu.make_async_copy(swap_ref, swaps_ref.at[i0], own_sem.at[2])
-    own_col.start()
-    own_sw.start()
     others(i0, lambda i: swap(i).start())
 
-    @pl.when(is_lead)
-    def _():
-        own_row = pltpu.make_async_copy(feat_ref.at[i0], rows_ref.at[i0, g0], own_sem.at[1])
-        own_row.start()
-        own_row.wait()
-        others(g0, lambda j: row2(i0, j).start())
-
-    own_col.wait()
-    others(i0, lambda i: col2(i, g0).start())
-
-    def forward_col(j):
-        col1_in(j).wait_recv()
-        others(i0, lambda i: col2(i, j).start())
-
-    others(g0, forward_col)
-
-    def forward_row(i):
-        @pl.when(i < n - 1)
+    def forward(k):
+        j = (g0 - i0 - k + 2 * n) % n
+        i = (i0 - g0 - k + 2 * n) % n
+
+        @pl.when(j != g0)
+        def _():
+            col1_in(j).wait_recv()
+            others(i0, lambda to: col2(to, j).start())
+
+        @pl.when((i != i0) & (i < n - 1))
         def _():
             row1_in(i).wait_recv()
-            others(g0, lambda j: row2(i, j).start())
-
-    others(i0, forward_row)
-
-    own_sw.wait()
+            others(g0, lambda to: row2(i, to).start())
+
+    def block(k, carry):
+        b = (i0 + g0 + k) % n
+
+        def tile(q, carry):
+            start = pl.multiple_of(b * width + q * LANES, LANES)
+            feat_ref[b, :, pl.ds(pl.multiple_of(q * LANES, LANES), LANES)] = feature_tile(x_ref, idx_ref, start)
+            return carry
+
+        lax.fori_loop(0, width // LANES, tile, 0)
+
+        @pl.when(b != g0)
+        def _():
+            col1(b).start()
+
+        @pl.when((b != i0) & is_lead)
+        def _():
+            row1(b).start()
+
+        @pl.when(b == g0)
+        def _():
+            cols_ref[i0, g0] = feat_ref[b]
+            others(i0, lambda to: col2(to, g0).start())
+
+        @pl.when((b == i0) & is_lead)
+        def _():
+            rows_ref[i0, g0] = feat_ref[b]
+            others(g0, lambda to: row2(i0, to).start())
+
+        @pl.when(k > 0)
+        def _():
+            forward(k - 1)
+
+        return carry
+
+    lax.fori_loop(0, n, block, 0)
+    forward(n - 1)
 
     def finish_swap(i):
         swap_in(i).wait_recv()
@@ -232,15 +263,7 @@
         feats = pair_index.shape[1]
         width = feats // n
         per = n * steps
-        x = jnp.swapaxes(archive[:, 0], 0, 1)
-        swap = jnp.broadcast_to(swap_history.T.reshape(1, per).astype(F32), (SUBLANES, per))
-        features = pl.pallas_call(
-            feature_kernel,
-            out_shape=jax.ShapeDtypeStruct((n, steps, width), BF16),
-            in_specs=vmem(2),
-            out_specs=vmem(1)[0],
-            compiler_params=pltpu.CompilerParams(vmem_limit_bytes=32 << 20),
-        )(x, pair_index)
+        raw = archive.reshape(steps * 3 * residues // LANES, LANES)
         dma = pltpu.SemaphoreType.DMA
         rows, cols, swaps = pl.pallas_call(
             functools.partial(exchange_kernel, n, n_rep),
@@ -249,14 +272,17 @@
                 jax.ShapeDtypeStruct((n, n, steps, width), BF16),
                 jax.ShapeDtypeStruct((n, SUBLANES, per), F32),
             ],
-            in_specs=vmem(2),
+            in_specs=[pl.BlockSpec(memory_space=pl.ANY)] * 2 + vmem(1),
             out_specs=vmem(3),
-            scratch_shapes=[dma((n,)), dma((n,)), dma((n,)), dma((n,)),
+            scratch_shapes=[pltpu.VMEM(raw.shape, F32), pltpu.VMEM(pair_index.shape, I32),
+                            pltpu.VMEM((3, steps, residues), F32), pltpu.VMEM((n, steps, width), BF16),
+                            pltpu.VMEM((SUBLANES, per), F32),
+                            dma((n,)), dma((n,)), dma((n,)), dma((n,)),
                             dma((n, n)), dma((n, n)), dma((n, n)), dma((n, n)),
-                            dma((n,)), dma((n,)), dma((3,))],
+                            dma((n,)), dma((n,)), dma((2,))],
             compiler_params=pltpu.CompilerParams(
                 collective_id=0, has_side_effects=True, vmem_limit_bytes=32 << 20),
-        )(features, swap)
+        )(raw, pair_index, swap_history.T)
         tile = min(256, width)
         shape = jax.ShapeDtypeStruct((width, width), F32)
         return pl.pallas_call(

time: 44.8 us -> 37.1 us (0.83)
  Pallas kernels: 40.7 us -> 33.7 us
  other arithmetic: 0.68 us -> 0 us
    pallas_call x1 -> x0, Pallas kernels: 16 us -> none  [local(): pl.pallas_call(feature_kernel, out_shape=jax.ShapeDtypeStruct((n, steps,...]
    pallas_call x1, Pallas kernels: 20.1 us -> 29.1 us  [local(): pl.pallas_call(functools.partial(exchange_kernel, n, n_rep), out_shape=[j...]
    convert_element_type x1 -> x0, other arithmetic: 0.68 us -> none  [local(): swap_history.T.reshape(1, per).astype(F32)]
    unnamed x3 -> x6, local copies, waits for them, and re-layouts: 2.34 us -> 2.56 us
where the time goes in v2:
time: 37.1 us; the launch traced here: 36.9 us
  Pallas kernels  33.7 us (91%)
  local copies, waits for them, and re-layouts  2.56 us (7%)
  between operations  0.65 us (2%)
    pallas_call x1, Pallas kernels, local(): pl.pallas_call(functools.partial(exchange_kernel, n, n_rep), out_shape=[j...  29.1 us
    pallas_call x1, Pallas kernels, local(): pl.pallas_call(functools.partial(covariance_kernel, (n - 1) * per), grid=...  4.57 us
    unnamed x6, local copies, waits for them, and re-layouts  2.56 us

profile of v2, /device:TPU:0, one launch (start us, length us, event | category | flops | bytes accessed | tf_op | source)
XLA Modules:
  0.0 36.9 jit_solution(3662281597361903767)
XLA Ops:
  0.6 0.0 copy-start
  0.6 1.1 %copy-done = f32[16,1,3,4096]{3,1,2,0:T(1,128)S(1)} copy-done((f32[16,1,3,4096]{3,1,2,0:T(1,128)S(1)}, f32[16,1,3,4096]{3,1,2,0:T(1,128)}, u32[]{:S(2)}) %copy-start) | copy-done | bytes 786456
  1.8 0.0 copy-start.1
  1.8 0.8 %copy-done.1 = s32[2,4096]{1,0:T(2,128)S(1)} copy-done((s32[2,4096]{1,0:T(2,128)S(1)}, s32[2,4096]{1,0:T(2,128)}, u32[]{:S(2)}) %copy-start.1) | copy-done | bytes 32792
  2.5 0.0 copy-start.2
  2.5 0.7 %copy-done.2 = s32[16,4]{0,1:T(4,128)S(1)} copy-done((s32[16,4]{0,1:T(4,128)S(1)}, s32[16,4]{0,1:T(4,128)}, u32[]{:S(2)}) %copy-start.2) | copy-done | bytes 280
  3.2 29.1 %shard_map.50 = (bf16[3,4,16,1024]{3,2,1,0:T(8,128)(2,1)S(1)}, bf16[4,4,16,1024]{3,2,1,0:T(8,128)(2,1)S(1)}, f32[4,8,64]{2,1,0:T(8,128)S(1)}) custom-call(f32[1536,128]{1,0:T(8,128)S(1)} %bitcast.4, s32[2,4096]{1,0:T(2,128)S(1)} %copy-done.1, s32[4,16]{1,0:T(4,128)S(1)} %bitcast.7), custom_call_target="tpu_custom_call" | custom-call | tf_op jit(solution)/shard_map/pallas_call | solution.py:268
  32.3 4.6 %shard_map.51 = (f32[1024,1024]{1,0:T(8,128)}, f32[1024,1024]{1,0:T(8,128)}) custom-call(bf16[3,64,1024]{2,1,0:T(8,128)(2,1)S(1)} %bitcast.6, bf16[4,64,1024]{2,1,0:T(8,128)(2,1)S(1)} %bitcast.5, f32[4,8,64]{2,1,0:T(8,128)S(1)} %get-tuple-element.7.swaps_ref), custom_call_target="tpu_custom_call" | custom-call | tf_op jit(solution)/shard_map/pallas_call | solution.py:288
Async XLA Ops:
  0.6 1.1 %copy-start = (f32[16,1,3,4096]{3,1,2,0:T(1,128)S(1)}, f32[16,1,3,4096]{3,1,2,0:T(1,128)}, u32[]{:S(2)}) copy-start(f32[16,1,3,4096]{3,1,2,0:T(1,128)} %param.3) | copy-start | bytes 2359300
  1.8 0.8 %copy-start.1 = (s32[2,4096]{1,0:T(2,128)S(1)}, s32[2,4096]{1,0:T(2,128)}, u32[]{:S(2)}) copy-start(s32[2,4096]{1,0:T(2,128)} %idx_hbm.1) | copy-start | bytes 98308
  2.5 0.7 %copy-start.2 = (s32[16,4]{0,1:T(4,128)S(1)}, s32[16,4]{0,1:T(4,128)}, u32[]{:S(2)}) copy-start(s32[16,4]{0,1:T(4,128)} %param.4) | copy-start | bytes 772

commit v3 on v2

--- a/solution.py
+++ b/solution.py
@@ -11,41 +11,39 @@
 DIST_FLOOR = 0.3
 LANES = 128
 SUBLANES = 8
+DEPTH = 256
+BF16_MAX = float(jnp.finfo(jnp.bfloat16).max)
 MESH = pl.DeviceIdType.MESH
 BF16, F32, I32 = jnp.bfloat16, jnp.float32, jnp.int32
 
 
-def lane_pick(table, lanes):
-    return jnp.take_along_axis(table, lanes, axis=1, mode="promise_in_bounds")
-
-
-def feature_tile(x_ref, idx_ref, start):
-    steps, residues = x_ref.shape[1:]
-    groups = [(c, t) for c in range(3) for t in range(0, steps, SUBLANES)]
-    lanes, chunks = [], []
-    for side in range(2):
-        index = jnp.broadcast_to(idx_ref[side : side + 1, pl.ds(start, LANES)], (SUBLANES, LANES))
-        lanes.append(lax.bitwise_and(index, LANES - 1))
-        chunks.append(lax.shift_right_logical(index, 7))
-    picked = [[None] * len(groups) for _ in range(2)]
-    for chunk in range(residues // LANES):
-        masks = [chunks[side] == chunk for side in range(2)]
-        for g, (c, t) in enumerate(groups):
-            table = x_ref[c, t : t + SUBLANES, chunk * LANES : (chunk + 1) * LANES]
-            for side in range(2):
-                found = lane_pick(table, lanes[side])
-                old = picked[side][g]
-                picked[side][g] = found if old is None else jnp.where(masks[side], found, old)
-    halves = steps // SUBLANES
-    out = []
-    for h in range(halves):
-        total = None
-        for c in range(3):
-            g = c * halves + h
-            diff = picked[0][g] - picked[1][g]
-            total = diff * diff if total is None else total + diff * diff
-        out.append(1.0 / jnp.maximum(jnp.sqrt(total), DIST_FLOOR))
-    return jnp.concatenate(out, axis=0).astype(BF16)
+def pieces(value):
+    high = jnp.clip(value, -BF16_MAX, BF16_MAX).astype(BF16)
+    rest = value - high.astype(F32)
+    middle = rest.astype(BF16)
+    return high, middle, (rest - middle.astype(F32)).astype(BF16)
+
+
+def feature_block(parts_ref, idx_ref, start, width, steps):
+    count, residues = parts_ref.shape
+    one, two = (idx_ref[side : side + 1, pl.ds(start, width)] for side in range(2))
+    same = one == two
+    one, two = jnp.where(same, -1, one), jnp.where(same, -1, two)
+    shape = (DEPTH, width)
+    residue = lax.broadcasted_iota(I32, shape, 0).astype(jnp.int16)
+    plus, zero = jnp.ones(shape, BF16), jnp.zeros(shape, BF16)
+    total = None
+    for first in range(0, residues, DEPTH):
+        at_one = residue == jnp.broadcast_to(one - first, shape).astype(jnp.int16)
+        at_two = residue == jnp.broadcast_to(two - first, shape).astype(jnp.int16)
+        chosen = jnp.where(at_one, plus, jnp.where(at_two, -plus, zero))
+        part = jnp.dot(parts_ref[:, first : first + DEPTH], chosen, preferred_element_type=F32)
+        total = part if total is None else total + part
+    third = count // 3
+    displace = total[:third] + total[third : 2 * third] + total[2 * third :]
+    square = displace * displace
+    square = square[:steps] + square[steps : 2 * steps] + square[2 * steps :]
+    return (1.0 / jnp.maximum(jnp.sqrt(square), DIST_FLOOR)).astype(BF16)
 
 
 def flat_swaps(swap):
@@ -61,7 +59,7 @@
 
 
 def exchange_kernel(n, n_rep, raw_ref, idx_hbm, swap_in_ref, rows_ref, cols_ref, swaps_ref,
-                    raw, idx_ref, x_ref, feat_ref, swap_ref,
+                    raw, idx_ref, parts_ref, feat_ref, swap_ref,
                     s_row1, r_row1, s_col1, r_col1, s_row2, r_row2, s_col2, r_col2, s_sw, r_sw, own_sem):
     i0 = lax.axis_index("tm")
     g0 = lax.axis_index("feat") * n_rep + lax.axis_index("rep")
@@ -123,15 +121,18 @@
 
     swap_ref[...] = flat_swaps(swap_in_ref[...])
     swaps_ref[i0] = swap_ref[...]
-    _, steps, residues = x_ref.shape
+    count, residues = parts_ref.shape
+    steps = feat_ref.shape[1]
     chunks = residues // LANES
     width = feat_ref.shape[2]
     get_raw.wait()
     for c in range(3):
-        for t in range(0, steps, SUBLANES):
-            for h in range(chunks):
-                x_ref[c, t : t + SUBLANES, h * LANES : (h + 1) * LANES] = raw[
-                    pl.ds((t * 3 + c) * chunks + h, SUBLANES, stride=3 * chunks), :]
+        for h in range(chunks):
+            rows = [raw[pl.ds((t * 3 + c) * chunks + h, SUBLANES, stride=3 * chunks), :]
+                    for t in range(0, steps, SUBLANES)]
+            for p, piece in enumerate(pieces(jnp.concatenate(rows, axis=0))):
+                top = (p * 3 + c) * steps
+                parts_ref[top : top + steps, h * LANES : (h + 1) * LANES] = piece
     get_idx.wait()
     pl.semaphore_wait(barrier, 2 * (n - 1))
     others(i0, lambda i: swap(i).start())
@@ -153,12 +154,8 @@
     def block(k, carry):
         b = (i0 + g0 + k) % n
 
-        def tile(q, carry):
-            start = pl.multiple_of(b * width + q * LANES, LANES)
-            feat_ref[b, :, pl.ds(pl.multiple_of(q * LANES, LANES), LANES)] = feature_tile(x_ref, idx_ref, start)
-            return carry
-
-        lax.fori_loop(0, width // LANES, tile, 0)
+        start = pl.multiple_of(b * width, LANES)
+        feat_ref[b] = feature_block(parts_ref, idx_ref, start, width, steps)
 
         @pl.when(b != g0)
         def _():
@@ -275,7 +272,7 @@
             in_specs=[pl.BlockSpec(memory_space=pl.ANY)] * 2 + vmem(1),
             out_specs=vmem(3),
             scratch_shapes=[pltpu.VMEM(raw.shape, F32), pltpu.VMEM(pair_index.shape, I32),
-                            pltpu.VMEM((3, steps, residues), F32), pltpu.VMEM((n, steps, width), BF16),
+                            pltpu.VMEM((9 * steps, residues), BF16), pltpu.VMEM((n, steps, width), BF16),
                             pltpu.VMEM((SUBLANES, per), F32),
                             dma((n,)), dma((n,)), dma((n,)), dma((n,)),
                             dma((n, n)), dma((n, n)), dma((n, n)), dma((n, n)),

time: 37.1 us -> 31.4 us (0.85)
  Pallas kernels: 33.7 us -> 28 us
    pallas_call x1, Pallas kernels: 29.1 us -> 23.4 us  [local(): pl.pallas_call(functools.partial(exchange_kernel, n, n_rep), out_shape=[j...]
where the time goes in v3:
time: 31.4 us; the launch traced here: 31.2 us
  Pallas kernels  28 us (89%)
  local copies, waits for them, and re-layouts  2.56 us (8%)
  between operations  0.65 us (2%)
    pallas_call x1, Pallas kernels, local(): pl.pallas_call(functools.partial(exchange_kernel, n, n_rep), out_shape=[j...  23.4 us
    pallas_call x1, Pallas kernels, local(): pl.pallas_call(functools.partial(covariance_kernel, (n - 1) * per), grid=...  4.57 us
    unnamed x6, local copies, waits for them, and re-layouts  2.56 us

profile of v3, /device:TPU:0, one launch (start us, length us, event | category | flops | bytes accessed | tf_op | source)
XLA Modules:
  0.0 31.2 jit_solution(12722633066018994107)
XLA Ops:
  0.6 0.0 copy-start
  0.6 1.1 %copy-done = f32[16,1,3,4096]{3,1,2,0:T(1,128)S(1)} copy-done((f32[16,1,3,4096]{3,1,2,0:T(1,128)S(1)}, f32[16,1,3,4096]{3,1,2,0:T(1,128)}, u32[]{:S(2)}) %copy-start) | copy-done | bytes 786456
  1.8 0.0 copy-start.1
  1.8 0.8 %copy-done.1 = s32[2,4096]{1,0:T(2,128)S(1)} copy-done((s32[2,4096]{1,0:T(2,128)S(1)}, s32[2,4096]{1,0:T(2,128)}, u32[]{:S(2)}) %copy-start.1) | copy-done | bytes 32792
  2.5 0.0 copy-start.2
  2.5 0.7 %copy-done.2 = s32[16,4]{0,1:T(4,128)S(1)} copy-done((s32[16,4]{0,1:T(4,128)S(1)}, s32[16,4]{0,1:T(4,128)}, u32[]{:S(2)}) %copy-start.2) | copy-done | bytes 280
  3.2 23.4 %shard_map.50 = (bf16[3,4,16,1024]{3,2,1,0:T(8,128)(2,1)S(1)}, bf16[4,4,16,1024]{3,2,1,0:T(8,128)(2,1)S(1)}, f32[4,8,64]{2,1,0:T(8,128)S(1)}) custom-call(f32[1536,128]{1,0:T(8,128)S(1)} %bitcast.4, s32[2,4096]{1,0:T(2,128)S(1)} %copy-done.1, s32[4,16]{1,0:T(4,128)S(1)} %bitcast.7), custom_call_target="tpu_custom_call" | custom-call | tf_op jit(solution)/shard_map/pallas_call | solution.py:265
  26.6 4.6 %shard_map.51 = (f32[1024,1024]{1,0:T(8,128)}, f32[1024,1024]{1,0:T(8,128)}) custom-call(bf16[3,64,1024]{2,1,0:T(8,128)(2,1)S(1)} %bitcast.6, bf16[4,64,1024]{2,1,0:T(8,128)(2,1)S(1)} %bitcast.5, f32[4,8,64]{2,1,0:T(8,128)S(1)} %get-tuple-element.7.swaps_ref), custom_call_target="tpu_custom_call" | custom-call | tf_op jit(solution)/shard_map/pallas_call | solution.py:285
Async XLA Ops:
  0.6 1.1 %copy-start = (f32[16,1,3,4096]{3,1,2,0:T(1,128)S(1)}, f32[16,1,3,4096]{3,1,2,0:T(1,128)}, u32[]{:S(2)}) copy-start(f32[16,1,3,4096]{3,1,2,0:T(1,128)} %param.3) | copy-start | bytes 2359300
  1.8 0.8 %copy-start.1 = (s32[2,4096]{1,0:T(2,128)S(1)}, s32[2,4096]{1,0:T(2,128)}, u32[]{:S(2)}) copy-start(s32[2,4096]{1,0:T(2,128)} %idx_hbm.1) | copy-start | bytes 98308
  2.5 0.7 %copy-start.2 = (s32[16,4]{0,1:T(4,128)S(1)}, s32[16,4]{0,1:T(4,128)}, u32[]{:S(2)}) copy-start(s32[16,4]{0,1:T(4,128)} %param.4) | copy-start | bytes 772

commit v4 on v3

--- a/solution.py
+++ b/solution.py
@@ -58,16 +58,18 @@
     return jnp.broadcast_to(row, (SUBLANES, per))
 
 
-def exchange_kernel(n, n_rep, raw_ref, idx_hbm, swap_in_ref, rows_ref, cols_ref, swaps_ref,
-                    raw, idx_ref, parts_ref, feat_ref, swap_ref,
-                    s_row1, r_row1, s_col1, r_col1, s_row2, r_row2, s_col2, r_col2, s_sw, r_sw, own_sem):
+def exchange_kernel(n, n_rep, raw_hbm, idx_hbm, swap_hbm, rows_ref, cols_ref, swaps_ref,
+                    raw, idx_ref, own_swap_ref, parts_ref, feat_ref, swap_ref,
+                    s_row1, r_row1, s_col1, r_col1, s_row2, r_row2, s_up, s_down, r_col2, s_sw, r_sw, own_sem):
     i0 = lax.axis_index("tm")
     g0 = lax.axis_index("feat") * n_rep + lax.axis_index("rep")
     is_lead = i0 < n - 1
-    get_raw = pltpu.make_async_copy(raw_ref, raw, own_sem.at[0])
+    get_raw = pltpu.make_async_copy(raw_hbm, raw, own_sem.at[0])
     get_idx = pltpu.make_async_copy(idx_hbm, idx_ref, own_sem.at[1])
     get_raw.start()
     get_idx.start()
+    get_swap = pltpu.make_async_copy(swap_hbm, own_swap_ref, own_sem.at[2])
+    get_swap.start()
 
     def time_id(i):
         return {"tm": i}
@@ -103,11 +105,38 @@
     def row2_in(i, j):
         return remote(rows_ref.at[i, j], rows_ref.at[i, j], s_row2.at[i, j], r_row2.at[i, j], group_id(j))
 
-    def col2(i, j):
-        return remote(cols_ref.at[i0, j], cols_ref.at[i0, j], s_col2.at[i, j], r_col2.at[i0, j], time_id(i))
+    def up(i, j):
+        return remote(cols_ref.at[i, j], cols_ref.at[i, j], s_up.at[i, j], r_col2.at[i, j], time_id(i0 + 1))
+
+    def down(i, j):
+        return remote(cols_ref.at[i, j], cols_ref.at[i, j], s_down.at[i, j], r_col2.at[i, j], time_id(i0 - 1))
 
     def col2_in(i, j):
-        return remote(cols_ref.at[i, j], cols_ref.at[i, j], s_col2.at[i, j], r_col2.at[i, j], time_id(i))
+        return remote(cols_ref.at[i, j], cols_ref.at[i, j], s_up.at[i, j], r_col2.at[i, j], time_id(i))
+
+    def spread(j):
+        @pl.when(i0 < n - 1)
+        def _():
+            up(i0, j).start()
+
+        @pl.when(i0 > 0)
+        def _():
+            down(i0, j).start()
+
+    def relay(k, hop):
+        below, above = i0 - hop, i0 + hop
+
+        @pl.when((below >= 0) & (i0 < n - 1))
+        def _():
+            j = (g0 - below - k + 2 * n) % n
+            col2_in(below, j).wait_recv()
+            up(below, j).start()
+
+        @pl.when((above < n) & (i0 > 0))
+        def _():
+            j = (g0 - above - k + 2 * n) % n
+            col2_in(above, j).wait_recv()
+            down(above, j).start()
 
     def swap(i):
         return remote(swap_ref, swaps_ref.at[i0], s_sw.at[i], r_sw.at[i0], time_id(i))
@@ -119,7 +148,8 @@
     others(i0, lambda i: pl.semaphore_signal(barrier, inc=1, device_id=time_id(i), device_id_type=MESH))
     others(g0, lambda j: pl.semaphore_signal(barrier, inc=1, device_id=group_id(j), device_id_type=MESH))
 
-    swap_ref[...] = flat_swaps(swap_in_ref[...])
+    get_swap.wait()
+    swap_ref[...] = flat_swaps(own_swap_ref[...])
     swaps_ref[i0] = swap_ref[...]
     count, residues = parts_ref.shape
     steps = feat_ref.shape[1]
@@ -144,7 +174,7 @@
         @pl.when(j != g0)
         def _():
             col1_in(j).wait_recv()
-            others(i0, lambda to: col2(to, j).start())
+            spread(j)
 
         @pl.when((i != i0) & (i < n - 1))
         def _():
@@ -168,7 +198,7 @@
         @pl.when(b == g0)
         def _():
             cols_ref[i0, g0] = feat_ref[b]
-            others(i0, lambda to: col2(to, g0).start())
+            spread(g0)
 
         @pl.when((b == i0) & is_lead)
         def _():
@@ -179,10 +209,29 @@
         def _():
             forward(k - 1)
 
+        def relays(hop, carry):
+            @pl.when(k - 1 - hop >= 0)
+            def _():
+                relay(k - 1 - hop, hop)
+            return carry
+
+        lax.fori_loop(1, n - 1, relays, 0)
         return carry
 
     lax.fori_loop(0, n, block, 0)
     forward(n - 1)
+
+    def late(k, carry):
+        def relays(hop, carry):
+            @pl.when((k - 1 - hop >= 0) & (k - 1 - hop < n))
+            def _():
+                relay(k - 1 - hop, hop)
+            return carry
+
+        lax.fori_loop(1, n - 1, relays, 0)
+        return carry
+
+    lax.fori_loop(n, 2 * n - 1, late, 0)
 
     def finish_swap(i):
         swap_in(i).wait_recv()
@@ -205,10 +254,21 @@
     lax.fori_loop(0, n - 1, end_rows, 0)
 
     def end_cols(j, carry):
-        def one(i):
-            col2(i, j).wait_send()
-            col2_in(i, j).wait_recv()
-        others(i0, one)
+        def end(i, carry):
+            @pl.when((i <= i0) & (i0 < n - 1))
+            def _():
+                up(i, j).wait_send()
+
+            @pl.when((i >= i0) & (i0 > 0))
+            def _():
+                down(i, j).wait_send()
+
+            @pl.when(((i < i0) & (i0 == n - 1)) | ((i > i0) & (i0 == 0)))
+            def _():
+                col2_in(i, j).wait_recv()
+            return carry
+
+        lax.fori_loop(0, n, end, 0)
         return carry
 
     lax.fori_loop(0, n, end_cols, 0)
@@ -269,14 +329,15 @@
                 jax.ShapeDtypeStruct((n, n, steps, width), BF16),
                 jax.ShapeDtypeStruct((n, SUBLANES, per), F32),
             ],
-            in_specs=[pl.BlockSpec(memory_space=pl.ANY)] * 2 + vmem(1),
+            in_specs=[pl.BlockSpec(memory_space=pltpu.HBM)] * 3,
             out_specs=vmem(3),
             scratch_shapes=[pltpu.VMEM(raw.shape, F32), pltpu.VMEM(pair_index.shape, I32),
+                            pltpu.VMEM(swap_history.shape[::-1], I32),
                             pltpu.VMEM((9 * steps, residues), BF16), pltpu.VMEM((n, steps, width), BF16),
                             pltpu.VMEM((SUBLANES, per), F32),
                             dma((n,)), dma((n,)), dma((n,)), dma((n,)),
-                            dma((n, n)), dma((n, n)), dma((n, n)), dma((n, n)),
-                            dma((n,)), dma((n,)), dma((2,))],
+                            dma((n, n)), dma((n, n)), dma((n, n)), dma((n, n)), dma((n, n)),
+                            dma((n,)), dma((n,)), dma((3,))],
             compiler_params=pltpu.CompilerParams(
                 collective_id=0, has_side_effects=True, vmem_limit_bytes=32 << 20),
         )(raw, pair_index, swap_history.T)

time: 31.4 us -> 34.7 us (1.11)
  Pallas kernels: 28 us -> 31.3 us
    pallas_call x1, Pallas kernels: 23.4 us -> 26.7 us  [local(): pl.pallas_call(functools.partial(exchange_kernel, n, n_rep), out_shape=[j...]
where the time goes in v4:
time: 34.7 us; the launch traced here: 34.5 us
  Pallas kernels  31.3 us (90%)
  local copies, waits for them, and re-layouts  2.56 us (7%)
  between operations  0.65 us (2%)
    pallas_call x1, Pallas kernels, local(): pl.pallas_call(functools.partial(exchange_kernel, n, n_rep), out_shape=[j...  26.7 us
    pallas_call x1, Pallas kernels, local(): pl.pallas_call(functools.partial(covariance_kernel, (n - 1) * per), grid=...  4.58 us
    unnamed x6, local copies, waits for them, and re-layouts  2.56 us

profile of v4, /device:TPU:0, one launch (start us, length us, event | category | flops | bytes accessed | tf_op | source)
XLA Modules:
  0.0 34.5 jit_solution(4444173731969968678)
XLA Ops:
  0.6 0.0 copy-start
  0.6 1.1 %copy-done = f32[16,1,3,4096]{3,1,2,0:T(1,128)S(1)} copy-done((f32[16,1,3,4096]{3,1,2,0:T(1,128)S(1)}, f32[16,1,3,4096]{3,1,2,0:T(1,128)}, u32[]{:S(2)}) %copy-start) | copy-done | bytes 786456
  1.8 0.0 copy-start.1
  1.8 0.8 %copy-done.1 = s32[2,4096]{1,0:T(2,128)S(1)} copy-done((s32[2,4096]{1,0:T(2,128)S(1)}, s32[2,4096]{1,0:T(2,128)}, u32[]{:S(2)}) %copy-start.1) | copy-done | bytes 32792
  2.5 0.0 copy-start.2
  2.5 0.7 %copy-done.2 = s32[16,4]{0,1:T(4,128)S(1)} copy-done((s32[16,4]{0,1:T(4,128)S(1)}, s32[16,4]{0,1:T(4,128)}, u32[]{:S(2)}) %copy-start.2) | copy-done | bytes 280
  3.2 26.7 %shard_map.50 = (bf16[3,4,16,1024]{3,2,1,0:T(8,128)(2,1)S(1)}, bf16[4,4,16,1024]{3,2,1,0:T(8,128)(2,1)S(1)}, f32[4,8,64]{2,1,0:T(8,128)S(1)}) custom-call(f32[1536,128]{1,0:T(8,128)S(1)} %bitcast.4, s32[2,4096]{1,0:T(2,128)S(1)} %copy-done.1, s32[4,16]{1,0:T(4,128)S(1)} %bitcast.7), custom_call_target="tpu_custom_call" | custom-call | tf_op jit(solution)/shard_map/pallas_call | solution.py:325
  29.9 4.6 %shard_map.51 = (f32[1024,1024]{1,0:T(8,128)}, f32[1024,1024]{1,0:T(8,128)}) custom-call(bf16[3,64,1024]{2,1,0:T(8,128)(2,1)S(1)} %bitcast.6, bf16[4,64,1024]{2,1,0:T(8,128)(2,1)S(1)} %bitcast.5, f32[4,8,64]{2,1,0:T(8,128)S(1)} %get-tuple-element.7.swaps_ref), custom_call_target="tpu_custom_call" | custom-call | tf_op jit(solution)/shard_map/pallas_call | solution.py:346
Async XLA Ops:
  0.6 1.1 %copy-start = (f32[16,1,3,4096]{3,1,2,0:T(1,128)S(1)}, f32[16,1,3,4096]{3,1,2,0:T(1,128)}, u32[]{:S(2)}) copy-start(f32[16,1,3,4096]{3,1,2,0:T(1,128)} %param.3) | copy-start | bytes 2359300
  1.8 0.8 %copy-start.1 = (s32[2,4096]{1,0:T(2,128)S(1)}, s32[2,4096]{1,0:T(2,128)}, u32[]{:S(2)}) copy-start(s32[2,4096]{1,0:T(2,128)} %idx_hbm.1) | copy-start | bytes 98308
  2.5 0.7 %copy-start.2 = (s32[16,4]{0,1:T(4,128)S(1)}, s32[16,4]{0,1:T(4,128)}, u32[]{:S(2)}) copy-start(s32[16,4]{0,1:T(4,128)} %param.4) | copy-start | bytes 772

commit v5 on v3

--- a/solution.py
+++ b/solution.py
@@ -58,16 +58,18 @@
     return jnp.broadcast_to(row, (SUBLANES, per))
 
 
-def exchange_kernel(n, n_rep, raw_ref, idx_hbm, swap_in_ref, rows_ref, cols_ref, swaps_ref,
-                    raw, idx_ref, parts_ref, feat_ref, swap_ref,
+def exchange_kernel(n, n_rep, raw_hbm, idx_hbm, swap_hbm, rows_ref, cols_ref, swaps_ref,
+                    raw, idx_ref, own_swap_ref, parts_ref, feat_ref, swap_ref,
                     s_row1, r_row1, s_col1, r_col1, s_row2, r_row2, s_col2, r_col2, s_sw, r_sw, own_sem):
     i0 = lax.axis_index("tm")
     g0 = lax.axis_index("feat") * n_rep + lax.axis_index("rep")
     is_lead = i0 < n - 1
-    get_raw = pltpu.make_async_copy(raw_ref, raw, own_sem.at[0])
+    get_raw = pltpu.make_async_copy(raw_hbm, raw, own_sem.at[0])
     get_idx = pltpu.make_async_copy(idx_hbm, idx_ref, own_sem.at[1])
     get_raw.start()
     get_idx.start()
+    get_swap = pltpu.make_async_copy(swap_hbm, own_swap_ref, own_sem.at[2])
+    get_swap.start()
 
     def time_id(i):
         return {"tm": i}
@@ -119,7 +121,8 @@
     others(i0, lambda i: pl.semaphore_signal(barrier, inc=1, device_id=time_id(i), device_id_type=MESH))
     others(g0, lambda j: pl.semaphore_signal(barrier, inc=1, device_id=group_id(j), device_id_type=MESH))
 
-    swap_ref[...] = flat_swaps(swap_in_ref[...])
+    get_swap.wait()
+    swap_ref[...] = flat_swaps(own_swap_ref[...])
     swaps_ref[i0] = swap_ref[...]
     count, residues = parts_ref.shape
     steps = feat_ref.shape[1]
@@ -138,21 +141,23 @@
     others(i0, lambda i: swap(i).start())
 
     def forward(k):
-        j = (g0 - i0 - k + 2 * n) % n
-        i = (i0 - g0 - k + 2 * n) % n
-
-        @pl.when(j != g0)
-        def _():
+        @pl.when(k > 0)
+        def _():
+            j = (g0 - k + n) % n
             col1_in(j).wait_recv()
             others(i0, lambda to: col2(to, j).start())
 
-        @pl.when((i != i0) & (i < n - 1))
-        def _():
-            row1_in(i).wait_recv()
-            others(g0, lambda to: row2(i, to).start())
+        @pl.when((g0 + k) % n == i0)
+        def _():
+            def one(i):
+                @pl.when(i < n - 1)
+                def _():
+                    row1_in(i).wait_recv()
+                    others(g0, lambda to: row2(i, to).start())
+            others(i0, one)
 
     def block(k, carry):
-        b = (i0 + g0 + k) % n
+        b = (g0 + k) % n
 
         start = pl.multiple_of(b * width, LANES)
         feat_ref[b] = feature_block(parts_ref, idx_ref, start, width, steps)
@@ -269,16 +274,17 @@
                 jax.ShapeDtypeStruct((n, n, steps, width), BF16),
                 jax.ShapeDtypeStruct((n, SUBLANES, per), F32),
             ],
-            in_specs=[pl.BlockSpec(memory_space=pl.ANY)] * 2 + vmem(1),
+            in_specs=[pl.BlockSpec(memory_space=pltpu.HBM)] * 3,
             out_specs=vmem(3),
             scratch_shapes=[pltpu.VMEM(raw.shape, F32), pltpu.VMEM(pair_index.shape, I32),
+                            pltpu.VMEM(swap_history.shape[::-1], I32),
                             pltpu.VMEM((9 * steps, residues), BF16), pltpu.VMEM((n, steps, width), BF16),
                             pltpu.VMEM((SUBLANES, per), F32),
                             dma((n,)), dma((n,)), dma((n,)), dma((n,)),
                             dma((n, n)), dma((n, n)), dma((n, n)), dma((n, n)),
-                            dma((n,)), dma((n,)), dma((2,))],
+                            dma((n,)), dma((n,)), dma((3,))],
             compiler_params=pltpu.CompilerParams(
-                collective_id=0, has_side_effects=True, vmem_limit_bytes=32 << 20),
+                collective_id=0, has_side_effects=True, vmem_limit_bytes=60 << 20),
         )(raw, pair_index, swap_history.T)
         tile = min(256, width)
         shape = jax.ShapeDtypeStruct((width, width), F32)
@@ -293,7 +299,7 @@
             ],
             out_specs=[pl.BlockSpec((tile, width), lambda r: (r, 0))] * 2,
             scratch_shapes=[pltpu.VMEM(((n - 1) * per, width), BF16), pltpu.VMEM((2, SUBLANES, width), F32)],
-            compiler_params=pltpu.CompilerParams(vmem_limit_bytes=48 << 20),
+            compiler_params=pltpu.CompilerParams(vmem_limit_bytes=60 << 20),
         )(rows.reshape(n - 1, per, width), cols.reshape(n, per, width), swaps)
 
     return jax.shard_map(

time: 31.4 us -> 31.5 us (level)
  the two profiles are of different devices: /device:TPU:0 before, /device:TPU:1 now
where the time goes in v5:
time: 31.5 us; the launch traced here: 31.3 us
  Pallas kernels  30.7 us (97%)
  between operations  0.64 us (2%)
    pallas_call x1, Pallas kernels, local(): pl.pallas_call(functools.partial(exchange_kernel, n, n_rep), out_shape=[j...  24.8 us
    pallas_call x1, Pallas kernels, local(): pl.pallas_call(functools.partial(covariance_kernel, (n - 1) * per), grid=...  5.95 us

profile of v5, /device:TPU:1, one launch (start us, length us, event | category | flops | bytes accessed | tf_op | source)
XLA Modules:
  0.0 31.3 jit_solution(8129814472887671999)
XLA Ops:
  0.6 24.8 %shard_map.50 = (bf16[3,4,16,1024]{3,2,1,0:T(8,128)(2,1)}, bf16[4,4,16,1024]{3,2,1,0:T(8,128)(2,1)}, f32[4,8,64]{2,1,0:T(8,128)}) custom-call(f32[1536,128]{1,0:T(8,128)} %bitcast.4, s32[2,4096]{1,0:T(2,128)} %idx_hbm.1, s32[4,16]{1,0:T(4,128)} %bitcast.7), custom_call_target="tpu_custom_call" | custom-call | tf_op jit(solution)/shard_map/pallas_call | solution.py:270
  25.4 5.9 %shard_map.51 = (f32[1024,1024]{1,0:T(8,128)}, f32[1024,1024]{1,0:T(8,128)}) custom-call(bf16[3,64,1024]{2,1,0:T(8,128)(2,1)} %bitcast.6, bf16[4,64,1024]{2,1,0:T(8,128)(2,1)} %bitcast.5, f32[4,8,64]{2,1,0:T(8,128)} %get-tuple-element.7.swaps_ref), custom_call_target="tpu_custom_call" | custom-call | tf_op jit(solution)/shard_map/pallas_call | solution.py:291

commit v6 on v5

--- a/solution.py
+++ b/solution.py
@@ -141,23 +141,21 @@
     others(i0, lambda i: swap(i).start())
 
     def forward(k):
-        @pl.when(k > 0)
-        def _():
-            j = (g0 - k + n) % n
+        j = (g0 - i0 - k + 2 * n) % n
+        i = (i0 - g0 - k + 2 * n) % n
+
+        @pl.when(j != g0)
+        def _():
             col1_in(j).wait_recv()
             others(i0, lambda to: col2(to, j).start())
 
-        @pl.when((g0 + k) % n == i0)
-        def _():
-            def one(i):
-                @pl.when(i < n - 1)
-                def _():
-                    row1_in(i).wait_recv()
-                    others(g0, lambda to: row2(i, to).start())
-            others(i0, one)
+        @pl.when((i != i0) & (i < n - 1))
+        def _():
+            row1_in(i).wait_recv()
+            others(g0, lambda to: row2(i, to).start())
 
     def block(k, carry):
-        b = (g0 + k) % n
+        b = (i0 + g0 + k) % n
 
         start = pl.multiple_of(b * width, LANES)
         feat_ref[b] = feature_block(parts_ref, idx_ref, start, width, steps)
@@ -286,7 +284,7 @@
             compiler_params=pltpu.CompilerParams(
                 collective_id=0, has_side_effects=True, vmem_limit_bytes=60 << 20),
         )(raw, pair_index, swap_history.T)
-        tile = min(256, width)
+        tile = min(LANES, width)
         shape = jax.ShapeDtypeStruct((width, width), F32)
         return pl.pallas_call(
             functools.partial(covariance_kernel, (n - 1) * per),

time: 31.5 us -> 33.4 us (1.060)
  the two profiles are of different devices: /device:TPU:1 before, /device:TPU:0 now
where the time goes in v6:
time: 33.4 us; the launch traced here: 32.9 us
  Pallas kernels  32.3 us (97%)
  between operations  0.64 us (2%)
    pallas_call x1, Pallas kernels, local(): pl.pallas_call(functools.partial(exchange_kernel, n, n_rep), out_shape=[j...  24.7 us
    pallas_call x1, Pallas kernels, local(): pl.pallas_call(functools.partial(covariance_kernel, (n - 1) * per), grid=...  7.58 us

profile of v6, /device:TPU:0, one launch (start us, length us, event | category | flops | bytes accessed | tf_op | source)
XLA Modules:
  0.0 32.9 jit_solution(13465918223417182381)
XLA Ops:
  0.6 24.7 %shard_map.50 = (bf16[3,4,16,1024]{3,2,1,0:T(8,128)(2,1)}, bf16[4,4,16,1024]{3,2,1,0:T(8,128)(2,1)}, f32[4,8,64]{2,1,0:T(8,128)}) custom-call(f32[1536,128]{1,0:T(8,128)} %bitcast.4, s32[2,4096]{1,0:T(2,128)} %idx_hbm.1, s32[4,16]{1,0:T(4,128)} %bitcast.7), custom_call_target="tpu_custom_call" | custom-call | tf_op jit(solution)/shard_map/pallas_call | solution.py:268
  25.3 7.6 %shard_map.51 = (f32[1024,1024]{1,0:T(8,128)}, f32[1024,1024]{1,0:T(8,128)}) custom-call(bf16[3,64,1024]{2,1,0:T(8,128)(2,1)} %bitcast.6, bf16[4,64,1024]{2,1,0:T(8,128)(2,1)} %bitcast.5, f32[4,8,64]{2,1,0:T(8,128)} %get-tuple-element.7.swaps_ref), custom_call_target="tpu_custom_call" | custom-call | tf_op jit(solution)/shard_map/pallas_call | solution.py:289

commit v7 on v3

--- a/solution.py
+++ b/solution.py
@@ -280,7 +280,7 @@
             compiler_params=pltpu.CompilerParams(
                 collective_id=0, has_side_effects=True, vmem_limit_bytes=32 << 20),
         )(raw, pair_index, swap_history.T)
-        tile = min(256, width)
+        tile = min(512, width)
         shape = jax.ShapeDtypeStruct((width, width), F32)
         return pl.pallas_call(
             functools.partial(covariance_kernel, (n - 1) * per),

time: 31.4 us -> 31.3 us (level)
  no operation moved by 1% of the time
where the time goes in v7:
time: 31.3 us; the launch traced here: 31 us
  Pallas kernels  27.8 us (89%)
  local copies, waits for them, and re-layouts  2.56 us (8%)
  between operations  0.65 us (2%)
    pallas_call x1, Pallas kernels, local(): pl.pallas_call(functools.partial(exchange_kernel, n, n_rep), out_shape=[j...  23.4 us
    pallas_call x1, Pallas kernels, local(): pl.pallas_call(functools.partial(covariance_kernel, (n - 1) * per), grid=...  4.38 us
    unnamed x6, local copies, waits for them, and re-layouts  2.56 us

profile of v7, /device:TPU:0, one launch (start us, length us, event | category | flops | bytes accessed | tf_op | source)
XLA Modules:
  0.0 31.0 jit_solution(7798821980488142043)
XLA Ops:
  0.6 0.0 copy-start
  0.6 1.1 %copy-done = f32[16,1,3,4096]{3,1,2,0:T(1,128)S(1)} copy-done((f32[16,1,3,4096]{3,1,2,0:T(1,128)S(1)}, f32[16,1,3,4096]{3,1,2,0:T(1,128)}, u32[]{:S(2)}) %copy-start) | copy-done | bytes 786456
  1.8 0.0 copy-start.1
  1.8 0.8 %copy-done.1 = s32[2,4096]{1,0:T(2,128)S(1)} copy-done((s32[2,4096]{1,0:T(2,128)S(1)}, s32[2,4096]{1,0:T(2,128)}, u32[]{:S(2)}) %copy-start.1) | copy-done | bytes 32792
  2.5 0.0 copy-start.2
  2.5 0.7 %copy-done.2 = s32[16,4]{0,1:T(4,128)S(1)} copy-done((s32[16,4]{0,1:T(4,128)S(1)}, s32[16,4]{0,1:T(4,128)}, u32[]{:S(2)}) %copy-start.2) | copy-done | bytes 280
  3.2 23.4 %shard_map.50 = (bf16[3,4,16,1024]{3,2,1,0:T(8,128)(2,1)S(1)}, bf16[4,4,16,1024]{3,2,1,0:T(8,128)(2,1)S(1)}, f32[4,8,64]{2,1,0:T(8,128)S(1)}) custom-call(f32[1536,128]{1,0:T(8,128)S(1)} %bitcast.4, s32[2,4096]{1,0:T(2,128)S(1)} %copy-done.1, s32[4,16]{1,0:T(4,128)S(1)} %bitcast.7), custom_call_target="tpu_custom_call" | custom-call | tf_op jit(solution)/shard_map/pallas_call | solution.py:265
  26.6 4.4 %shard_map.51 = (f32[1024,1024]{1,0:T(8,128)}, f32[1024,1024]{1,0:T(8,128)}) custom-call(bf16[3,64,1024]{2,1,0:T(8,128)(2,1)S(1)} %bitcast.6, bf16[4,64,1024]{2,1,0:T(8,128)(2,1)S(1)} %bitcast.5, f32[4,8,64]{2,1,0:T(8,128)S(1)} %get-tuple-element.7.swaps_ref), custom_call_target="tpu_custom_call" | custom-call | tf_op jit(solution)/shard_map/pallas_call | solution.py:285
Async XLA Ops:
  0.6 1.1 %copy-start = (f32[16,1,3,4096]{3,1,2,0:T(1,128)S(1)}, f32[16,1,3,4096]{3,1,2,0:T(1,128)}, u32[]{:S(2)}) copy-start(f32[16,1,3,4096]{3,1,2,0:T(1,128)} %param.3) | copy-start | bytes 2359300
  1.8 0.8 %copy-start.1 = (s32[2,4096]{1,0:T(2,128)S(1)}, s32[2,4096]{1,0:T(2,128)}, u32[]{:S(2)}) copy-start(s32[2,4096]{1,0:T(2,128)} %idx_hbm.1) | copy-start | bytes 98308
  2.5 0.7 %copy-start.2 = (s32[16,4]{0,1:T(4,128)S(1)}, s32[16,4]{0,1:T(4,128)}, u32[]{:S(2)}) copy-start(s32[16,4]{0,1:T(4,128)} %param.4) | copy-start | bytes 772
